TPU v7x, 32 devices: a whole 2x2x4 slice. The times are simulated.
32 devices in a mesh: subtree: 2 (over x), panel: 4 (over y, core), snap: 4 (over z).
Axes of the slice: x: 2, y: 2, z: 4, core: 2. Of those that a mesh axis runs over, the one named last changes fastest.
Arguments:
- leaf_rhs: bfloat16 [8, 1024, 128], P('subtree', 'panel', 'snap'), may hold values from -6 to 6
- upper_rhs: bfloat16 [7, 1024, 128], P(None, 'panel', 'snap'), may hold values from -6 to 6
- leaf_inv: bfloat16 [8, 1024, 1024], P('subtree', 'panel'), may hold values from -1 to 2, as said below
- upper_inv: bfloat16 [7, 1024, 1024], P(None, 'panel'), may hold values from -1 to 2, as said below
- leaf_panels: bfloat16 [8, 3, 1024, 1024], P('subtree', None, 'panel'), may hold values from -0.09375 to 0.09375
- mid_panels: bfloat16 [4, 2, 1024, 1024], P(None, None, 'panel'), may hold values from -0.09375 to 0.09375
- top_panels: bfloat16 [2, 1024, 1024], P(None, 'panel'), may hold values from -0.09375 to 0.09375
- leaf_widths: int32 [8], P('subtree'), may hold values from 256 to 1024
- upper_widths: int32 [7], replicated, may hold values from 256 to 1024
Outputs:
- leaf_solution: bfloat16 [8, 1024, 128], P('subtree', 'panel', 'snap')
- upper_solution: bfloat16 [7, 1024, 128], P(None, 'panel', 'snap')
Inputs may be any that keep to these rules, and one draw needn't show every extreme that they name: `leaf_inv`: each inverse block is a full matrix near the identity. `upper_inv`: each inverse block is a full matrix near the identity.
All inputs are finite; a program needn't handle non-finite values.
Results may differ from a plain program's by a relative error of at most 0.024.
Values may be sent and summed in bfloat16 or wider, within the bound.
A program may use at most 64 MiB of HBM per device.

v0:
```python
import jax
import jax.numpy as jnp
from jax import lax
from jax.sharding import PartitionSpec as P


def live_mask(widths, full_width):
    return (jnp.arange(full_width, dtype=jnp.int32)[None, :] < widths[:, None]).astype(jnp.float32)


def own_rows(mask_full, own_count):
    return lax.dynamic_slice_in_dim(mask_full, lax.axis_index("panel") * own_count, own_count, 1)


def solve_down(inverse, reduced, mask_full):
    own_count = inverse.shape[1]
    live_cols = mask_full.astype(jnp.bfloat16)
    result = jnp.einsum(
        "nrw,nwc->nrc",
        inverse,
        lax.all_gather(reduced, "panel", axis=1, tiled=True) * live_cols[:, :, None],
        preferred_element_type=jnp.float32,
    )
    return (result * own_rows(mask_full, own_count)[:, :, None]).astype(jnp.bfloat16)


def spread(panels, solved):
    return jnp.einsum(
        "nkrw,nwc->nkrc",
        panels,
        lax.all_gather(solved, "panel", axis=1, tiled=True),
        preferred_element_type=jnp.float32,
    )


def ancestor_tables(global_index, level, count_up):
    offsets = [0, 0, 4, 6]
    slot_ids = jnp.arange(7, dtype=jnp.int32)
    tables = []
    for ancestor_rank in range(count_up):
        target = offsets[level + 1 + ancestor_rank] + jnp.right_shift(
            global_index, 1 + ancestor_rank
        )
        tables.append((slot_ids[None, :] == target[:, None]).astype(jnp.float32))
    return tables


def add_coupled(accum, coupled, tables):
    for ancestor_rank in range(len(tables)):
        accum = accum + jnp.einsum(
            "nrc,nu->urc",
            coupled[:, ancestor_rank],
            tables[ancestor_rank],
            precision=lax.Precision.HIGHEST,
        )
    return accum


def solve_up(inverse, panels, solved, upper_x, tables, mask_full):
    own_count = inverse.shape[1]
    if panels is None:
        reduced = solved
    else:
        picked = jnp.stack(
            [
                jnp.einsum(
                    "nu,urc->nrc",
                    table.astype(jnp.bfloat16),
                    upper_x,
                    preferred_element_type=jnp.float32,
                ).astype(jnp.bfloat16)
                for table in tables
            ],
            axis=1,
        )
        carried = lax.psum_scatter(
            jnp.einsum("nkrw,nkrc->wnc", panels, picked, preferred_element_type=jnp.float32).astype(
                jnp.bfloat16
            ),
            "panel",
            scatter_dimension=0,
            tiled=True,
        ).astype(jnp.float32)
        reduced = (solved.astype(jnp.float32) - jnp.transpose(carried, (1, 0, 2))).astype(
            jnp.bfloat16
        )
    own_live = own_rows(mask_full, own_count)
    masked = reduced * own_live[:, :, None].astype(jnp.bfloat16)
    summed = lax.psum_scatter(
        jnp.einsum("nrw,nrc->wnc", inverse, masked, preferred_element_type=jnp.float32).astype(
            jnp.bfloat16
        ),
        "panel",
        scatter_dimension=0,
        tiled=True,
    ).astype(jnp.float32)
    return (jnp.transpose(summed, (1, 0, 2)) * own_live[:, :, None]).astype(jnp.bfloat16)


def per_device(
    leaf_rhs,
    upper_rhs,
    leaf_inv,
    upper_inv,
    leaf_panels,
    mid_panels,
    top_panels,
    leaf_widths,
    upper_widths,
):
    full_width = leaf_inv.shape[2]
    own_count = leaf_inv.shape[1]
    leaf_count = leaf_inv.shape[0]
    groups = lax.axis_size("subtree")
    group_id = lax.axis_index("subtree")
    leaf_live = live_mask(leaf_widths, full_width)
    upper_live = live_mask(upper_widths, full_width)
    leaf_index = group_id * leaf_count + jnp.arange(leaf_count, dtype=jnp.int32)
    upper_index = jnp.arange(7, dtype=jnp.int32)
    leaf_tables = ancestor_tables(leaf_index, 0, 3)
    mid_tables = ancestor_tables(upper_index[0:4], 1, 2)
    high_tables = ancestor_tables(upper_index[4:6] - 4, 2, 1)
    top_stack = top_panels[:, None]
    leaf_sol = solve_down(leaf_inv, leaf_rhs, leaf_live)
    coupled_sum = jnp.zeros((7, own_count, leaf_rhs.shape[2]), jnp.float32)
    coupled_sum = add_coupled(coupled_sum, spread(leaf_panels, leaf_sol), leaf_tables)
    column_share = leaf_rhs.shape[2] // groups
    coupled_sum = lax.psum_scatter(
        coupled_sum.astype(jnp.bfloat16), "subtree", scatter_dimension=2, tiled=True
    ).astype(jnp.float32)
    upper_part = lax.dynamic_slice_in_dim(upper_rhs, group_id * column_share, column_share, 2)
    mid_sol = solve_down(
        upper_inv[0:4],
        (upper_part[0:4].astype(jnp.float32) - coupled_sum[0:4]).astype(jnp.bfloat16),
        upper_live[0:4],
    )
    coupled_sum = add_coupled(coupled_sum, spread(mid_panels, mid_sol), mid_tables)
    high_sol = solve_down(
        upper_inv[4:6],
        (upper_part[4:6].astype(jnp.float32) - coupled_sum[4:6]).astype(jnp.bfloat16),
        upper_live[4:6],
    )
    coupled_sum = add_coupled(coupled_sum, spread(top_stack, high_sol), high_tables)
    root_sol = solve_down(
        upper_inv[6:7],
        (upper_part[6:7].astype(jnp.float32) - coupled_sum[6:7]).astype(jnp.bfloat16),
        upper_live[6:7],
    )
    column_count = upper_part.shape[2]
    zero_mid = jnp.zeros((4, own_count, column_count), jnp.bfloat16)
    zero_high = jnp.zeros((2, own_count, column_count), jnp.bfloat16)
    root_x = solve_up(upper_inv[6:7], None, root_sol, None, None, upper_live[6:7])
    upper_x = jnp.concatenate([zero_mid, zero_high, root_x], axis=0)
    high_x = solve_up(upper_inv[4:6], top_stack, high_sol, upper_x, high_tables, upper_live[4:6])
    upper_x = jnp.concatenate([zero_mid, high_x, root_x], axis=0)
    mid_x = solve_up(upper_inv[0:4], mid_panels, mid_sol, upper_x, mid_tables, upper_live[0:4])
    upper_x = jnp.concatenate([mid_x, high_x, root_x], axis=0)
    upper_x = lax.all_gather(upper_x, "subtree", axis=2, tiled=True)
    leaf_x = solve_up(leaf_inv, leaf_panels, leaf_sol, upper_x, leaf_tables, leaf_live)
    return (leaf_x, upper_x)


def solution(mesh):
    in_specs = (
        P("subtree", "panel", "snap"),
        P(None, "panel", "snap"),
        P("subtree", "panel", None),
        P(None, "panel", None),
        P("subtree", None, "panel", None),
        P(None, None, "panel", None),
        P(None, "panel", None),
        P("subtree"),
        P(),
    )
    out_specs = (P("subtree", "panel", "snap"), P(None, "panel", "snap"))
    return jax.shard_map(
        per_device, mesh=mesh, in_specs=in_specs, out_specs=out_specs, check_vma=False
    )
```

profile of v0, /device:TPU:0, one launch (start us, length us, event | category | flops | bytes accessed | tf_op | source)
XLA Modules:
  0.0 253.7 jit_solution(11947335732800104918)
XLA Ops:
  7.2 0.0 reduce-scatter.9.cloned.1.call-start
  7.3 0.9 fusion.93
  8.1 7.4 %all_gather.24 = bf16[4,1024,32]{1,2,0:T(8,128)(2,1)S(1)} all-gather(bf16[4,256,32]{1,2,0:T(8,128)(2,1)} %param.9), channel_id=1, replica_groups=mesh['subtree'=2,'panel'=4,'snap'=4] {'panel'}, dimensions={1}, use_global_device_ids=true | all-gather | bytes 327680 | tf_op jit(solution)/shard_map/all_gather | solution.py:21
  15.6 0.7 fusion.22
  16.3 5.9 %all_gather.25 = bf16[4,1024,32]{1,2,0:T(8,128)(2,1)S(1)} all-gather(bf16[4,256,32]{1,2,0:T(8,128)(2,1)S(1)} %fusion.22), channel_id=1, replica_groups=mesh['subtree'=2,'panel'=4,'snap'=4] {'panel'}, dimensions={1}, use_global_device_ids=true | all-gather | bytes 327680 | tf_op jit(solution)/shard_map/all_gather | solution.py:31
  22.1 4.8 %convolution_bitcast_fusion.1 = f32[4,3,256,32]{2,3,1,0:T(8,128)S(1)} fusion(bf16[4,3,256,1024]{3,2,1,0:T(8,128)(2,1)} %param.13, bf16[4,1024,32]{1,2,0:T(8,128)(2,1)S(1)} %all_gather.25), kind=kOutput, calls=%fused_computation.7 | convolution fusion | flops 201326592 | bytes 6946816 | tf_op jit(solution)/shard_map/nkrw,nwc->nkrc/dot_general | solution.py:28
  27.0 0.4 fusion.54
  27.4 0.4 convolution_add_fusion.1
  27.8 1.1 fusion.7
  28.8 0.0 reduce-scatter.9.cloned.1.call-update
  28.9 0.0 reduce-scatter.11.cloned.1.call-start
  28.9 0.1 fusion.87
  29.2 0.1 shift-right-arithmetic_add_fusion
  29.3 11.3 %reduce-scatter.9.cloned.1.call-done = bf16[7,256,16]{1,0,2:T(8,128)(2,1)} async-done(((bf16[7,256,32]{1,0,2:T(8,128)(2,1)}), bf16[7,256,16]{1,0,2:T(8,128)(2,1)}) %reduce-scatter.9.cloned.1.call-update) | async-done | bytes 57360 | tf_op jit(solution)/shard_map/reduce_scatter | solution.py:128
  40.6 0.8 convert_element_type.246
  41.5 5.4 %all_gather.26 = bf16[4,1024,16]{1,0,2:T(4,128)(2,1)S(1)} all-gather(bf16[4,256,16]{1,0,2:T(4,128)(2,1)S(1)} %fusion.64), channel_id=1, replica_groups=mesh['subtree'=2,'panel'=4,'snap'=4] {'panel'}, dimensions={1}, use_global_device_ids=true | all-gather | bytes 163840 | tf_op jit(solution)/shard_map/all_gather | solution.py:21
  46.9 2.3 fusion.32
  49.2 5.6 %all_gather.27 = bf16[4,1024,16]{1,2,0:T(8,128)(2,1)S(1)} all-gather(bf16[4,256,16]{1,2,0:T(8,128)(2,1)S(1)} %fusion.32), channel_id=1, replica_groups=mesh['subtree'=2,'panel'=4,'snap'=4] {'panel'}, dimensions={1}, use_global_device_ids=true | all-gather | bytes 163840 | tf_op jit(solution)/shard_map/all_gather | solution.py:31
  54.8 3.4 %convolution_bitcast_fusion.3 = f32[4,2,256,16]{2,3,1,0:T(8,128)S(1)} fusion(bf16[4,2,256,1024]{3,2,1,0:T(8,128)(2,1)} %param.14, bf16[4,1024,16]{1,2,0:T(8,128)(2,1)S(1)} %all_gather.27), kind=kOutput, calls=%fused_computation.18 | convolution fusion | flops 67108864 | bytes 4456448 | tf_op jit(solution)/shard_map/nkrw,nwc->nkrc/dot_general | solution.py:28
  58.2 0.3 convolution_add_fusion.3
  58.5 0.3 convolution_add_fusion.2
  58.9 5.3 %all_gather.28 = bf16[2,1024,16]{1,0,2:T(2,128)(2,1)S(1)} all-gather(bf16[2,256,16]{1,0,2:T(2,128)(2,1)S(1)} %fusion.73), channel_id=1, replica_groups=mesh['subtree'=2,'panel'=4,'snap'=4] {'panel'}, dimensions={1}, use_global_device_ids=true | all-gather | bytes 81920 | tf_op jit(solution)/shard_map/all_gather | solution.py:21
  64.2 1.6 fusion.36
  65.8 5.2 %all_gather.29 = bf16[2,1024,16]{1,2,0:T(8,128)(2,1)S(1)} all-gather(bf16[2,256,16]{1,2,0:T(8,128)(2,1)S(1)} %fusion.36), channel_id=1, replica_groups=mesh['subtree'=2,'panel'=4,'snap'=4] {'panel'}, dimensions={1}, use_global_device_ids=true | all-gather | bytes 81920 | tf_op jit(solution)/shard_map/all_gather | solution.py:31
  71.0 0.4 fusion.142
  71.4 0.3 fusion.83
  71.8 5.3 %all_gather.30 = bf16[1,1024,16]{1,0,2:T(2,128)(2,1)S(1)} all-gather(bf16[1,256,16]{1,0,2:T(2,128)(2,1)S(1)} %fusion.94), channel_id=1, replica_groups=mesh['subtree'=2,'panel'=4,'snap'=4] {'panel'}, dimensions={1}, use_global_device_ids=true | all-gather | bytes 40960 | tf_op jit(solution)/shard_map/all_gather | solution.py:21
  77.0 0.1 broadcast_multiply_fusion.1
  77.1 2.4 fusion.31
  79.5 0.0 reduce-scatter.11.cloned.1.call-update
  79.5 0.0 reduce-scatter.13.cloned.1.call-start
  79.6 0.1 fusion.141
  79.6 19.4 %reduce-scatter.11.cloned.1.call-done = bf16[256,1,16]{0,2,1:T(8,128)(2,1)} async-done(((bf16[1024,1,16]{0,2,1:T(8,128)(2,1)}), bf16[256,1,16]{0,2,1:T(8,128)(2,1)}) %reduce-scatter.11.cloned.1.call-update) | async-done | bytes 8208 | tf_op jit(solution)/shard_map/reduce_scatter | solution.py:89
  99.0 0.7 fusion.91
  99.7 0.2 fusion.61
  99.9 0.1 copy.42
  100.1 0.9 fusion.21
  101.0 0.0 reduce-scatter.15.cloned.1.call-start
  101.1 20.6 %reduce-scatter.13.cloned.1.call-done = bf16[256,2,16]{0,2,1:T(8,128)(2,1)} async-done(((bf16[1024,2,16]{0,2,1:T(8,128)(2,1)}), bf16[256,2,16]{0,2,1:T(8,128)(2,1)}) %reduce-scatter.13.cloned.1.call-update) | async-done | bytes 16400 | tf_op jit(solution)/shard_map/reduce_scatter | solution.py:76
  121.6 2.1 fusion.17
  123.8 0.0 reduce-scatter.17.cloned.1.call-start
  123.8 20.1 %reduce-scatter.15.cloned.1.call-done = bf16[256,2,16]{0,2,1:T(8,128)(2,1)} async-done(((bf16[1024,2,16]{0,2,1:T(8,128)(2,1)}), bf16[256,2,16]{0,2,1:T(8,128)(2,1)}) %reduce-scatter.15.cloned.1.call-update) | async-done | bytes 16400 | tf_op jit(solution)/shard_map/reduce_scatter | solution.py:89
  143.9 0.7 fusion.81
  144.7 0.2 fusion.29
  144.9 0.2 fusion.30
  145.2 3.5 %fusion.15 = bf16[1024,4,16]{0,2,1:T(8,128)(2,1)} fusion(bf16[4,2,256,1024]{3,2,1,0:T(8,128)(2,1)} %param.14, bf16[4,2,256,16]{2,0,3,1:T(4,128)(2,1)S(1)} %pad_maximum_fusion.4), kind=kOutput, calls=%fused_computation.21 | convolution fusion | flops 67174400 | bytes 4390912 | tf_op jit(solution)/shard_map/nkrw,nkrc->wnc/dot_general | solution.py:77
  148.7 0.0 reduce-scatter.19.cloned.1.call-start
  148.7 19.7 %reduce-scatter.17.cloned.1.call-done = bf16[256,4,16]{0,2,1:T(8,128)(2,1)} async-done(((bf16[1024,4,16]{0,2,1:T(8,128)(2,1)}), bf16[256,4,16]{0,2,1:T(8,128)(2,1)}) %reduce-scatter.17.cloned.1.call-update) | async-done | bytes 32784 | tf_op jit(solution)/shard_map/reduce_scatter | solution.py:76
  168.4 2.6 %fusion.12 = bf16[1024,4,16]{0,2,1:T(8,128)(2,1)} fusion(bf16[7,256,1024]{2,1,0:T(8,128)(2,1)} %param.12, bf16[256,4,16]{0,2,1:T(8,128)(2,1)} %reduce-scatter.17.cloned.1.call-done, bf16[4,256,16]{1,2,0:T(8,128)(2,1)S(1)} %fusion.32, bf16[4,256]{1,0:T(4,128)(2,1)S(1)} %get-tuple-element.4), kind=kOutput, calls=%fused_computation.20 | convolution fusion | flops 33701888 | bytes 2295808 | tf_op jit(solution)/shard_map/nrw,nrc->wnc/dot_general | solution.py:90
  171.1 0.0 reduce-scatter.21.cloned.1.call-start
  171.1 19.7 %reduce-scatter.19.cloned.1.call-done = bf16[256,4,16]{0,2,1:T(8,128)(2,1)} async-done(((bf16[1024,4,16]{0,2,1:T(8,128)(2,1)}), bf16[256,4,16]{0,2,1:T(8,128)(2,1)}) %reduce-scatter.19.cloned.1.call-update) | async-done | bytes 32784 | tf_op jit(solution)/shard_map/reduce_scatter | solution.py:89
  190.8 0.8 fusion.65
  191.6 4.9 %all_gather.31 = bf16[7,256,32]{1,2,0:T(8,128)(2,1)S(1)} all-gather(bf16[7,256,16]{1,2,0:T(8,128)(2,1)S(1)} %pad_maximum_fusion.5), channel_id=1, replica_groups=mesh['subtree'=2,'panel'=4,'snap'=4] {'subtree'}, dimensions={2}, use_global_device_ids=true | all-gather | bytes 172032 | tf_op jit(solution)/shard_map/all_gather | solution.py:158
  196.4 0.2 fusion.18
  196.7 0.2 fusion.19
  196.9 0.2 fusion.20
  197.1 0.2 pad_maximum_fusion
  197.3 4.7 %fusion.5 = bf16[1024,4,32]{0,2,1:T(8,128)(2,1)} fusion(bf16[4,3,256,1024]{3,2,1,0:T(8,128)(2,1)} %param.13, bf16[4,3,256,32]{2,0,3,1:T(4,128)(2,1)S(1)} %pad_maximum_fusion), kind=kOutput, calls=%fused_computation.8 | convolution fusion | flops 201457664 | bytes 6750208 | tf_op jit(solution)/shard_map/nkrw,nkrc->wnc/dot_general | solution.py:77
  202.0 0.0 reduce-scatter.23.cloned.1.call-start
  202.1 20.1 %reduce-scatter.21.cloned.1.call-done = bf16[256,4,32]{0,2,1:T(8,128)(2,1)} async-done(((bf16[1024,4,32]{0,2,1:T(8,128)(2,1)}), bf16[256,4,32]{0,2,1:T(8,128)(2,1)}) %reduce-scatter.21.cloned.1.call-update) | async-done | bytes 65552 | tf_op jit(solution)/shard_map/reduce_scatter | solution.py:76
  222.2 2.0 fusion.6
  224.2 20.5 %reduce-scatter.23.cloned.1.call-done = bf16[256,4,32]{0,2,1:T(8,128)(2,1)} async-done(((bf16[1024,4,32]{0,2,1:T(8,128)(2,1)}), bf16[256,4,32]{0,2,1:T(8,128)(2,1)}) %reduce-scatter.23.cloned.1.call-update) | async-done | bytes 65552 | tf_op jit(solution)/shard_map/reduce_scatter | solution.py:89
  244.8 1.5 fusion.49
  246.2 0.6 copy.93
  (50 shorter events, 0.6 us)
Async XLA Ops:
  7.2 8.4 %copy-start = (bf16[4,256,1024]{2,1,0:T(8,128)(2,1)S(1)}, bf16[4,256,1024]{2,1,0:T(8,128)(2,1)}, u32[]{:S(2)}) copy-start(bf16[4,256,1024]{2,1,0:T(8,128)(2,1)} %param.11) | copy-start | bytes 6291460
  7.2 33.4 %reduce-scatter.9.cloned.1.call-start = ((), (), s32[]{:S(2)}) async-start(), calls=%async_computation.8 | async-start | bytes 196608 | tf_op jit(solution)/shard_map/reduce_scatter | solution.py:128
  22.1 6.8 %copy-start.4 = (s32[7]{0:T(128)S(1)}, s32[7]{0:T(128)}, u32[]{:S(2)}) copy-start(s32[7]{0:T(128)} %param.17) | copy-start | bytes 88
  22.1 6.9 %copy-start.3 = (bf16[7,256,32]{1,2,0:T(8,128)(2,1)S(1)}, bf16[7,256,32]{1,2,0:T(8,128)(2,1)}, u32[]{:S(2)}) copy-start(bf16[7,256,32]{1,2,0:T(8,128)(2,1)} %param.10) | copy-start | bytes 344068
  28.9 70.1 %reduce-scatter.11.cloned.1.call-start = ((), (), s32[]{:S(2)}) async-start(), calls=%async_computation.9 | async-start | bytes 40960 | tf_op jit(solution)/shard_map/reduce_scatter | solution.py:89
  46.9 11.3 %copy-start.2 = (bf16[7,256,16]{1,0,2:T(8,128)(2,1)S(1)}, bf16[7,256,16]{1,0,2:T(8,128)(2,1)}, u32[]{:S(2)}) copy-start(bf16[7,256,16]{1,0,2:T(8,128)(2,1)} %reduce-scatter.9.cloned.1.call-done) | copy-start | bytes 172036
  49.2 21.8 %copy-start.1 = (bf16[2,256,1024]{2,1,0:T(8,128)(2,1)S(1)}, bf16[2,256,1024]{2,1,0:T(8,128)(2,1)}, u32[]{:S(2)}) copy-start(bf16[2,256,1024]{2,1,0:T(8,128)(2,1)} %param.15) | copy-start | bytes 3145732
  79.5 42.1 %reduce-scatter.13.cloned.1.call-start = ((), (), s32[]{:S(2)}) async-start(), calls=%async_computation.10 | async-start | bytes 81920 | tf_op jit(solution)/shard_map/reduce_scatter | solution.py:76
  101.0 42.9 %reduce-scatter.15.cloned.1.call-start = ((), (), s32[]{:S(2)}) async-start(), calls=%async_computation.11 | async-start | bytes 81920 | tf_op jit(solution)/shard_map/reduce_scatter | solution.py:89
  123.8 44.6 %reduce-scatter.17.cloned.1.call-start = ((), (), s32[]{:S(2)}) async-start(), calls=%async_computation.12 | async-start | bytes 163840 | tf_op jit(solution)/shard_map/reduce_scatter | solution.py:76
  148.7 42.1 %reduce-scatter.19.cloned.1.call-start = ((), (), s32[]{:S(2)}) async-start(), calls=%async_computation.13 | async-start | bytes 163840 | tf_op jit(solution)/shard_map/reduce_scatter | solution.py:89
  171.1 51.1 %reduce-scatter.21.cloned.1.call-start = ((), (), s32[]{:S(2)}) async-start(), calls=%async_computation.14 | async-start | bytes 327680 | tf_op jit(solution)/shard_map/reduce_scatter | solution.py:76
  202.0 42.7 %reduce-scatter.23.cloned.1.call-start = ((), (), s32[]{:S(2)}) async-start(), calls=%async_computation.15 | async-start | bytes 327680 | tf_op jit(solution)/shard_map/reduce_scatter | solution.py:89
Sparse Core Ops, SparseCore 0:
  29.0 11.5 reduce-scatter.8
  79.6 19.3 reduce-scatter.10
  102.1 19.4 reduce-scatter.12
  124.5 19.4 reduce-scatter.14
  148.8 19.5 reduce-scatter.16
  171.2 19.5 reduce-scatter.18
  202.1 20.0 reduce-scatter.20
  224.7 20.0 reduce-scatter.22
where the time goes:
time: 255 us; the launch traced here: 254 us
  waiting for transfers between devices  151 us (59%)
  blocking collectives  44.9 us (18%)
  matrix products  35.5 us (14%)
  between operations  14.5 us (6%)
  other arithmetic  6.07 us (2%)
    reduce_scatter x4, waiting for transfers between devices, solve_up(): lax.psum_scatter(jnp.einsum('nrw,nrc->wnc', inverse, masked, preferred_el...  79.6 us
    reduce_scatter x3, waiting for transfers between devices, solve_up(): lax.psum_scatter(jnp.einsum('nkrw,nkrc->wnc', panels, picked, preferred_e...  60.4 us
    all_gather x4, blocking collectives, solve_down(): lax.all_gather(reduced, 'panel', axis=1, tiled=True) * live_cols[:, :, None]  23.4 us
    all_gather x3, blocking collectives, spread(): lax.all_gather(solved, 'panel', axis=1, tiled=True)  16.7 us
    reduce_scatter x1, waiting for transfers between devices, per_device(): lax.psum_scatter(coupled_sum.astype(jnp.bfloat16), 'subtree', scatter_dim...  11.3 us
    dot_general x4, matrix products, solve_up(): jnp.einsum('nrw,nrc->wnc', inverse, masked, preferred_element_type=jnp.fl...  9.13 us
    dot_general x3, matrix products, solve_up(): jnp.einsum('nkrw,nkrc->wnc', panels, picked, preferred_element_type=jnp.f...  9.09 us
    dot_general x3, matrix products, spread(): jnp.einsum('nkrw,nwc->nkrc', panels, lax.all_gather(solved, 'panel', axis...  8.51 us
  transfers between devices with their start and end apart: 8, of which 8 were waited for; matrix products, arithmetic and copies ran while one was open for 0% of the time, Pallas kernels for 0%

commit v1 on v0

--- a/solution.py
+++ b/solution.py
@@ -2,6 +2,13 @@
 import jax.numpy as jnp
 from jax import lax
 from jax.sharding import PartitionSpec as P
+from jax.lax import axis_index, axis_size, ppermute
+
+
+def time_the_panel(vals, in_dim):
+    carry = list(vals.shape[1:])
+    carry[in_dim] *= vals.shape[0]
+    return jnp.moveaxis(vals, 0, in_dim).reshape(carry)
 
 
 def live_mask(widths, full_width):
@@ -15,10 +22,34 @@
 def solve_down(inverse, reduced, mask_full):
     own_count = inverse.shape[1]
     live_cols = mask_full.astype(jnp.bfloat16)
+
+    def _solve_positions(local_values, lane_axis, dim_at):
+        num_devices = axis_size(lane_axis)
+        by_rank = [(dd, (dd + 1) % num_devices) for dd in range(num_devices)]
+        small, arr_now = ([], [])
+        grid = [(p, tick) for tick, p in by_rank]
+        for no in range(num_devices - 1):
+            if no % 2 == 0:
+                small.append(
+                    ppermute(
+                        small[-1] if small else local_values, axis_name=lane_axis, perm=by_rank
+                    )
+                )
+            else:
+                arr_now.append(
+                    ppermute(
+                        arr_now[-1] if arr_now else local_values, axis_name=lane_axis, perm=grid
+                    )
+                )
+        y2 = jnp.stack([*small[::-1], local_values, *arr_now], axis=0)
+        local_out = axis_index(lane_axis) - len(small)
+        y2 = y2[(jnp.arange(num_devices) - local_out) % num_devices]
+        return time_the_panel(y2, dim_at)
+
     result = jnp.einsum(
         "nrw,nwc->nrc",
         inverse,
-        lax.all_gather(reduced, "panel", axis=1, tiled=True) * live_cols[:, :, None],
+        _solve_positions(reduced, "panel", 1) * live_cols[:, :, None],
         preferred_element_type=jnp.float32,
     )
     return (result * own_rows(mask_full, own_count)[:, :, None]).astype(jnp.bfloat16)

time: 255 us -> 277 us (1.086)
  blocking collectives: 44.9 us -> 22.6 us
  local copies, waits for them, and re-layouts: 1.02 us -> 20.5 us
  waiting for transfers between devices: 151 us -> 164 us
  starting transfers between devices: 0.33 us -> 9.14 us
  other arithmetic: 6.07 us -> 9.13 us
    all_gather x4 -> x0, blocking collectives: 23.4 us -> none  [solve_down(): lax.all_gather(reduced, 'panel', axis=1, tiled=True) * live_cols[:, :, None]]
    reduce_scatter x4 -> x3, waiting for transfers between devices: 79.6 us -> 59.5 us  [solve_up(): lax.psum_scatter(jnp.einsum('nrw,nrc->wnc', inverse, masked, preferred_el...]
    unnamed x8 -> x9, waiting for transfers between devices: 0.13 us -> 20.3 us
    unnamed x13 -> x50, local copies, waits for them, and re-layouts: 0.69 us -> 15.2 us
    ppermute x0 -> x12, waiting for transfers between devices: none -> 14.4 us  [the longest x8 14.2 us: _solve_positions(): ppermute(small[-1] if small else local_values, axis_name=lane_axis, perm=...]
    ppermute x0 -> x12, starting transfers between devices: none -> 8.63 us  [the longest x4 6.61 us: _solve_positions(): ppermute(arr_now[-1] if arr_now else local_values, axis_name=lane_axis, p...]
  transfers between devices with their start and end apart: 8 -> 20, of which waited for: 8 -> 17; matrix products, arithmetic and copies ran while one was open for 0% -> 2% of each run, Pallas kernels for 0% -> 0%
where the time goes in v1:
time: 277 us; the launch traced here: 276 us
  waiting for transfers between devices  164 us (59%)
  matrix products  36 us (13%)
  blocking collectives  22.6 us (8%)
  local copies, waits for them, and re-layouts  20.5 us (7%)
  between operations  14.7 us (5%)
  starting transfers between devices  9.14 us (3%)
  other arithmetic  9.13 us (3%)
    reduce_scatter x3, waiting for transfers between devices, solve_up(): lax.psum_scatter(jnp.einsum('nkrw,nkrc->wnc', panels, picked, preferred_e...  59.8 us
    reduce_scatter x3, waiting for transfers between devices, solve_up(): lax.psum_scatter(jnp.einsum('nrw,nrc->wnc', inverse, masked, preferred_el...  59.5 us
    unnamed x9, waiting for transfers between devices  20.3 us
    all_gather x3, blocking collectives, spread(): lax.all_gather(solved, 'panel', axis=1, tiled=True)  17.8 us
    unnamed x50, local copies, waits for them, and re-layouts  15.2 us
    ppermute x8, waiting for transfers between devices, _solve_positions(): ppermute(small[-1] if small else local_values, axis_name=lane_axis, perm=...  14.2 us
    reduce_scatter x1, waiting for transfers between devices, per_device(): lax.psum_scatter(coupled_sum.astype(jnp.bfloat16), 'subtree', scatter_dim...  9.73 us
    dot_general x3, matrix products, solve_up(): jnp.einsum('nkrw,nkrc->wnc', panels, picked, preferred_element_type=jnp.f...  9.05 us
  transfers between devices with their start and end apart: 20, of which 17 were waited for; matrix products, arithmetic and copies ran while one was open for 2% of the time, Pallas kernels for 0%

profile of v1, /device:TPU:0, one launch (start us, length us, event | category | flops | bytes accessed | tf_op | source)
XLA Modules:
  0.0 275.8 jit_solution(2212084545742403092)
XLA Ops:
  7.2 0.5 collective-permute-start
  7.7 2.0 collective-permute-start.2
  9.8 0.7 fusion.89
  10.5 0.7 fusion.82
  11.3 0.6 fusion.136
  11.9 0.7 collective-permute-start.1
  12.6 3.1 %collective-permute-done.1 = bf16[4,256,32]{1,2,0:T(8,128)(2,1)S(1)} collective-permute-done((bf16[4,256,32]{1,2,0:T(8,128)(2,1)S(1)}, bf16[4,256,32]{1,2,0:T(8,128)(2,1)S(1)}, u32[]{:S(2)}, u32[]{:S(2)}) %collective-permute-start.1) | collective-permute-done | bytes 65568 | tf_op jit(solution)/shard_map/ppermute | solution.py:34
  15.6 0.9 pad_maximum_fusion
  16.5 0.6 gather_fusion
  17.1 0.7 fusion.22
  17.8 7.1 %all_gather.12 = bf16[4,1024,32]{1,2,0:T(8,128)(2,1)S(1)} all-gather(bf16[4,256,32]{1,2,0:T(8,128)(2,1)S(1)} %fusion.22), channel_id=1, replica_groups=mesh['subtree'=2,'panel'=4,'snap'=4] {'panel'}, dimensions={1}, use_global_device_ids=true | all-gather | bytes 327680 | tf_op jit(solution)/shard_map/all_gather | solution.py:62
  24.9 4.7 %convolution_bitcast_fusion.1 = f32[4,3,256,32]{2,3,1,0:T(8,128)S(1)} fusion(bf16[4,3,256,1024]{3,2,1,0:T(8,128)(2,1)} %param.13, bf16[4,1024,32]{1,2,0:T(8,128)(2,1)S(1)} %all_gather.12), kind=kOutput, calls=%fused_computation.11 | convolution fusion | flops 201326592 | bytes 6946816 | tf_op jit(solution)/shard_map/nkrw,nwc->nkrc/dot_general | solution.py:59
  30.1 0.4 convolution_add_fusion.1
  30.6 1.1 fusion.7
  31.7 0.8 constant_dynamic-slice_fusion.1
  32.5 0.5 shift-right-arithmetic_add_fusion.1
  33.0 9.7 %reduce-scatter.11.cloned.1.call-done = bf16[7,256,16]{1,0,2:T(8,128)(2,1)} async-done(((bf16[7,256,32]{1,0,2:T(8,128)(2,1)}), bf16[7,256,16]{1,0,2:T(8,128)(2,1)}) %reduce-scatter.11.cloned.1.call-update) | async-done | bytes 57360 | tf_op jit(solution)/shard_map/reduce_scatter | solution.py:159
  42.8 0.8 convert_element_type.246
  43.7 0.6 shift-right-arithmetic_add_fusion
  44.3 1.7 collective-permute-start.5
  46.0 1.0 collective-permute-done.3
  47.0 0.7 constant_dynamic-slice_fusion
  47.8 2.6 collective-permute-done.4
  50.5 0.7 gather_fusion.1
  51.4 2.2 fusion.32
  53.6 5.4 %all_gather.13 = bf16[4,1024,16]{1,2,0:T(8,128)(2,1)S(1)} all-gather(bf16[4,256,16]{1,2,0:T(8,128)(2,1)S(1)} %fusion.32), channel_id=1, replica_groups=mesh['subtree'=2,'panel'=4,'snap'=4] {'panel'}, dimensions={1}, use_global_device_ids=true | all-gather | bytes 163840 | tf_op jit(solution)/shard_map/all_gather | solution.py:62
  59.1 3.5 %convolution_bitcast_fusion.3 = f32[4,2,256,16]{2,3,1,0:T(8,128)S(1)} fusion(bf16[4,2,256,1024]{3,2,1,0:T(8,128)(2,1)} %param.14, bf16[4,1024,16]{1,2,0:T(8,128)(2,1)S(1)} %all_gather.13), kind=kOutput, calls=%fused_computation.22 | convolution fusion | flops 67108864 | bytes 4456448 | tf_op jit(solution)/shard_map/nkrw,nwc->nkrc/dot_general | solution.py:59
  63.7 0.7 constant_dynamic-slice_fusion.5
  64.4 1.4 collective-permute-start.8
  65.8 0.7 collective-permute-done.6
  66.5 0.6 fusion.138
  67.2 2.4 collective-permute-done.7
  69.8 0.8 gather_fusion.2
  70.7 1.6 fusion.36
  72.3 5.2 %all_gather.14 = bf16[2,1024,16]{1,2,0:T(8,128)(2,1)S(1)} all-gather(bf16[2,256,16]{1,2,0:T(8,128)(2,1)S(1)} %fusion.36), channel_id=1, replica_groups=mesh['subtree'=2,'panel'=4,'snap'=4] {'panel'}, dimensions={1}, use_global_device_ids=true | all-gather | bytes 81920 | tf_op jit(solution)/shard_map/all_gather | solution.py:62
  77.9 0.9 fusion.78
  79.3 1.5 collective-permute-start.11
  80.8 1.3 collective-permute-done.9
  82.2 3.0 %collective-permute-done.10 = bf16[1,256,16]{1,0,2:T(2,128)(2,1)S(1)} collective-permute-done((bf16[1,256,16]{1,0,2:T(2,128)(2,1)S(1)}, bf16[1,256,16]{1,0,2:T(2,128)(2,1)S(1)}, u32[]{:S(2)}, u32[]{:S(2)}) %collective-permute-start.10) | collective-permute-done | bytes 8224 | tf_op jit(solution)/shard_map/ppermute | solution.py:34
  85.3 0.7 gather_fusion.3
  86.0 2.4 fusion.31
  88.6 19.3 %reduce-scatter.13.cloned.1.call-done = bf16[256,1,16]{0,2,1:T(8,128)(2,1)} async-done(((bf16[1024,1,16]{0,2,1:T(8,128)(2,1)}), bf16[256,1,16]{0,2,1:T(8,128)(2,1)}) %reduce-scatter.13.cloned.1.call-update) | async-done | bytes 8208 | tf_op jit(solution)/shard_map/reduce_scatter | solution.py:120
  107.9 0.7 fusion.86
  108.6 0.8 convolution_convert_fusion.9
  109.4 0.9 fusion.17
  110.6 19.9 %reduce-scatter.15.cloned.1.call-done = bf16[256,2,16]{0,2,1:T(8,128)(2,1)} async-done(((bf16[1024,2,16]{0,2,1:T(8,128)(2,1)}), bf16[256,2,16]{0,2,1:T(8,128)(2,1)}) %reduce-scatter.15.cloned.1.call-update) | async-done | bytes 16400 | tf_op jit(solution)/shard_map/reduce_scatter | solution.py:107
  130.5 1.5 fusion.18
  132.0 4.8 %copy.108 = bf16[1024,2,16]{1,2,0:T(8,128)(2,1)} copy(bf16[1024,2,16]{0,2,1:T(8,128)(2,1)S(1)} %fusion.18) | data formatting | bytes 131072
  136.8 6.5 %reshape.302 = bf16[1024,32]{1,0:T(8,128)(2,1)} reshape(bf16[1024,16,2]{2,1,0:T(8,128)(2,1)} %bitcast.206) | data formatting | bytes 131072
  143.4 20.1 %reduce-scatter.25.cloned.1.call-done = bf16[256,32]{1,0:T(8,128)(2,1)} async-done(((bf16[1024,32]{1,0:T(8,128)(2,1)}), bf16[256,32]{1,0:T(8,128)(2,1)}) %reduce-scatter.25.cloned.1.call-update) | async-done | bytes 16400
  163.5 2.2 reshape.303
  165.7 0.9 copy.109
  167.2 3.5 %fusion.15 = bf16[1024,4,16]{0,2,1:T(8,128)(2,1)} fusion(bf16[4,2,256,1024]{3,2,1,0:T(8,128)(2,1)} %param.14, bf16[4,2,256,16]{2,0,3,1:T(4,128)(2,1)S(1)} %pad_maximum_fusion.7), kind=kOutput, calls=%fused_computation.25 | convolution fusion | flops 67174400 | bytes 4390912 | tf_op jit(solution)/shard_map/nkrw,nkrc->wnc/dot_general | solution.py:108
  170.8 19.7 %reduce-scatter.17.cloned.1.call-done = bf16[256,4,16]{0,2,1:T(8,128)(2,1)} async-done(((bf16[1024,4,16]{0,2,1:T(8,128)(2,1)}), bf16[256,4,16]{0,2,1:T(8,128)(2,1)}) %reduce-scatter.17.cloned.1.call-update) | async-done | bytes 32784 | tf_op jit(solution)/shard_map/reduce_scatter | solution.py:107
  190.5 2.6 fusion.12
  193.2 19.7 %reduce-scatter.19.cloned.1.call-done = bf16[256,4,16]{0,2,1:T(8,128)(2,1)} async-done(((bf16[1024,4,16]{0,2,1:T(8,128)(2,1)}), bf16[256,4,16]{0,2,1:T(8,128)(2,1)}) %reduce-scatter.19.cloned.1.call-update) | async-done | bytes 32784 | tf_op jit(solution)/shard_map/reduce_scatter | solution.py:120
  212.9 0.8 fusion.63
  213.7 4.9 %all_gather.15 = bf16[7,256,32]{1,2,0:T(8,128)(2,1)S(1)} all-gather(bf16[7,256,16]{1,2,0:T(8,128)(2,1)S(1)} %pad_maximum_fusion.8), channel_id=1, replica_groups=mesh['subtree'=2,'panel'=4,'snap'=4] {'subtree'}, dimensions={2}, use_global_device_ids=true | all-gather | bytes 172032 | tf_op jit(solution)/shard_map/all_gather | solution.py:189
  219.4 4.7 %fusion.5 = bf16[1024,4,32]{0,2,1:T(8,128)(2,1)} fusion(bf16[4,3,256,1024]{3,2,1,0:T(8,128)(2,1)} %param.13, bf16[4,3,256,32]{2,0,3,1:T(4,128)(2,1)S(1)} %pad_maximum_fusion.1), kind=kOutput, calls=%fused_computation.12 | convolution fusion | flops 201457664 | bytes 6750208 | tf_op jit(solution)/shard_map/nkrw,nkrc->wnc/dot_general | solution.py:108
  224.2 20.2 %reduce-scatter.21.cloned.1.call-done = bf16[256,4,32]{0,2,1:T(8,128)(2,1)} async-done(((bf16[1024,4,32]{0,2,1:T(8,128)(2,1)}), bf16[256,4,32]{0,2,1:T(8,128)(2,1)}) %reduce-scatter.21.cloned.1.call-update) | async-done | bytes 65552 | tf_op jit(solution)/shard_map/reduce_scatter | solution.py:107
  244.3 2.0 fusion.6
  246.4 20.5 %reduce-scatter.23.cloned.1.call-done = bf16[256,4,32]{0,2,1:T(8,128)(2,1)} async-done(((bf16[1024,4,32]{0,2,1:T(8,128)(2,1)}), bf16[256,4,32]{0,2,1:T(8,128)(2,1)}) %reduce-scatter.23.cloned.1.call-update) | async-done | bytes 65552 | tf_op jit(solution)/shard_map/reduce_scatter | solution.py:120
  266.9 1.5 fusion.49
  268.3 0.6 copy.161
  (120 shorter events, 5.5 us)
Async XLA Ops:
  7.2 9.9 %copy-start = (bf16[4,256,1024]{2,1,0:T(8,128)(2,1)S(1)}, bf16[4,256,1024]{2,1,0:T(8,128)(2,1)}, u32[]{:S(2)}) copy-start(bf16[4,256,1024]{2,1,0:T(8,128)(2,1)} %param.11) | copy-start | bytes 6291460
  7.2 35.6 %reduce-scatter.11.cloned.1.call-start = ((), (), s32[]{:S(2)}) async-start(), calls=%async_computation.8 | async-start | bytes 196608 | tf_op jit(solution)/shard_map/reduce_scatter | solution.py:159
  7.2 4.6 %collective-permute-start = (bf16[4,256,32]{1,2,0:T(8,128)(2,1)}, bf16[4,256,32]{1,2,0:T(8,128)(2,1)S(1)}, u32[]{:S(2)}, u32[]{:S(2)}) collective-permute-start(bf16[4,256,32]{1,2,0:T(8,128)(2,1)} %param.9), channel_id=1, source_target_pairs={{0,4},{4,8},{8,12},{12,0},{1,5},{5,9},{9,13},{13,1},{2,6},{6,10},{... | collective-permute-start | bytes 196616 | tf_op jit(solution)/shard_map/ppermute | solution.py:34
  7.7 4.8 %collective-permute-start.2 = (bf16[4,256,32]{1,2,0:T(8,128)(2,1)}, bf16[4,256,32]{1,2,0:T(8,128)(2,1)S(1)}, u32[]{:S(2)}, u32[]{:S(2)}) collective-permute-start(bf16[4,256,32]{1,2,0:T(8,128)(2,1)} %param.9), channel_id=1, source_target_pairs={{4,0},{8,4},{12,8},{0,12},{5,1},{9,5},{13,9},{1,13},{6,2},{10,6},{... | collective-permute-start | bytes 196616 | tf_op jit(solution)/shard_map/ppermute | solution.py:40
  9.8 40.7 %copy-start.7 = (s32[1024]{0:T(1024)}, s32[1024]{0:T(1024)S(1)}, u32[]{:S(2)}) copy-start(s32[1024]{0:T(1024)S(1)} %pad_clamp_fusion) | copy-start | bytes 12292
  11.8 17.8 %copy-start.3 = (f32[4,256]{1,0:T(4,128)}, f32[4,256]{1,0:T(4,128)S(1)}, u32[]{:S(2)}) copy-start(f32[4,256]{1,0:T(4,128)S(1)} %get-tuple-element.3) | copy-start | bytes 12292
  11.8 39.5 %copy-start.5 = (f32[4,256]{1,0:T(4,128)}, f32[4,256]{1,0:T(4,128)S(1)}, u32[]{:S(2)}) copy-start(f32[4,256]{1,0:T(4,128)S(1)} %get-tuple-element.20) | copy-start | bytes 12292
  11.8 17.9 %copy-start.10 = (s32[4]{0:T(128)}, s32[4]{0:T(128)S(1)}, u32[]{:S(2)}) copy-start(s32[4]{0:T(128)S(1)} %get-tuple-element.22) | copy-start | bytes 52
  11.9 18.3 %copy-start.14 = (s32[4]{0:T(128)}, s32[4]{0:T(128)S(1)}, u32[]{:S(2)}) copy-start(s32[4]{0:T(128)S(1)} %get-tuple-element.21) | copy-start | bytes 52
  11.9 3.7 %collective-permute-start.1 = (bf16[4,256,32]{1,2,0:T(8,128)(2,1)S(1)}, bf16[4,256,32]{1,2,0:T(8,128)(2,1)S(1)}, u32[]{:S(2)}, u32[]{:S(2)}) collective-permute-start(bf16[4,256,32]{1,2,0:T(8,128)(2,1)S(1)} %collective-permute-done), channel_id=1, source_target_pairs={{0,4},{4,8},{8,12},{12,0},{1,5},{5,9},{9,13},{13,1},{2,6},{6,10},{... | collective-permute-start | bytes 196616 | tf_op jit(solution)/shard_map/ppermute | solution.py:34
  12.5 18.0 %copy-start.12 = (s32[4]{0:T(128)}, s32[4]{0:T(128)S(1)}, u32[]{:S(2)}) copy-start(s32[4]{0:T(128)S(1)} %shift-right-arithmetic_add_fusion.3) | copy-start | bytes 52
  31.7 76.2 %reduce-scatter.13.cloned.1.call-start = ((), (), s32[]{:S(2)}) async-start(), calls=%async_computation.9 | async-start | bytes 40960 | tf_op jit(solution)/shard_map/reduce_scatter | solution.py:120
  33.0 29.5 %copy-start.16 = (s32[4]{0:T(128)}, s32[4]{0:T(128)S(1)}, u32[]{:S(2)}) copy-start(s32[4]{0:T(128)S(1)} %get-tuple-element.16) | copy-start | bytes 52
  43.6 3.4 %collective-permute-start.3 = (bf16[4,256,16]{1,0,2:T(4,128)(2,1)S(1)}, bf16[4,256,16]{1,0,2:T(4,128)(2,1)S(1)}, u32[]{:S(2)}, u32[]{:S(2)}) collective-permute-start(bf16[4,256,16]{1,0,2:T(4,128)(2,1)S(1)} %fusion.62), channel_id=1, source_target_pairs={{0,4},{4,8},{8,12},{12,0},{1,5},{5,9},{9,13},{13,1},{2,6},{6,10},{... | collective-permute-start | bytes 98312 | tf_op jit(solution)/shard_map/ppermute | solution.py:34
  44.3 3.5 %collective-permute-start.5 = (bf16[4,256,16]{1,0,2:T(4,128)(2,1)S(1)}, bf16[4,256,16]{1,0,2:T(4,128)(2,1)S(1)}, u32[]{:S(2)}, u32[]{:S(2)}) collective-permute-start(bf16[4,256,16]{1,0,2:T(4,128)(2,1)S(1)} %fusion.62), channel_id=1, source_target_pairs={{4,0},{8,4},{12,8},{0,12},{5,1},{9,5},{13,9},{1,13},{6,2},{10,6},{... | collective-permute-start | bytes 98312 | tf_op jit(solution)/shard_map/ppermute | solution.py:40
  47.0 3.3 %collective-permute-start.4 = (bf16[4,256,16]{1,0,2:T(4,128)(2,1)S(1)}, bf16[4,256,16]{1,0,2:T(4,128)(2,1)S(1)}, u32[]{:S(2)}, u32[]{:S(2)}) collective-permute-start(bf16[4,256,16]{1,0,2:T(4,128)(2,1)S(1)} %collective-permute-done.3), channel_id=1, source_target_pairs={{0,4},{4,8},{8,12},{12,0},{1,5},{5,9},{9,13},{13,1},{2,6},{6,10},{... | collective-permute-start | bytes 98312 | tf_op jit(solution)/shard_map/ppermute | solution.py:34
  51.4 11.2 %copy-start.2 = (bf16[7,256,16]{1,0,2:T(8,128)(2,1)S(1)}, bf16[7,256,16]{1,0,2:T(8,128)(2,1)}, u32[]{:S(2)}) copy-start(bf16[7,256,16]{1,0,2:T(8,128)(2,1)} %reduce-scatter.11.cloned.1.call-done) | copy-start | bytes 172036
  51.4 11.5 %copy-start.18 = (s32[4]{0:T(128)S(1)}, s32[4]{0:T(128)}, u32[]{:S(2)}) copy-start(s32[4]{0:T(128)} %get-tuple-element.15) | copy-start | bytes 52
  59.1 18.5 %copy-start.1 = (bf16[2,256,1024]{2,1,0:T(8,128)(2,1)S(1)}, bf16[2,256,1024]{2,1,0:T(8,128)(2,1)}, u32[]{:S(2)}) copy-start(bf16[2,256,1024]{2,1,0:T(8,128)(2,1)} %param.15) | copy-start | bytes 3145732
  63.3 3.2 %collective-permute-start.6 = (bf16[2,256,16]{1,0,2:T(2,128)(2,1)S(1)}, bf16[2,256,16]{1,0,2:T(2,128)(2,1)S(1)}, u32[]{:S(2)}, u32[]{:S(2)}) collective-permute-start(bf16[2,256,16]{1,0,2:T(2,128)(2,1)S(1)} %fusion.72), channel_id=1, source_target_pairs={{0,4},{4,8},{8,12},{12,0},{1,5},{5,9},{9,13},{13,1},{2,6},{6,10},{... | collective-permute-start | bytes 49160 | tf_op jit(solution)/shard_map/ppermute | solution.py:34
  64.4 2.8 %collective-permute-start.8 = (bf16[2,256,16]{1,0,2:T(2,128)(2,1)S(1)}, bf16[2,256,16]{1,0,2:T(2,128)(2,1)S(1)}, u32[]{:S(2)}, u32[]{:S(2)}) collective-permute-start(bf16[2,256,16]{1,0,2:T(2,128)(2,1)S(1)} %fusion.72), channel_id=1, source_target_pairs={{4,0},{8,4},{12,8},{0,12},{5,1},{9,5},{13,9},{1,13},{6,2},{10,6},{... | collective-permute-start | bytes 49160 | tf_op jit(solution)/shard_map/ppermute | solution.py:40
  66.5 3.2 %collective-permute-start.7 = (bf16[2,256,16]{1,0,2:T(2,128)(2,1)S(1)}, bf16[2,256,16]{1,0,2:T(2,128)(2,1)S(1)}, u32[]{:S(2)}, u32[]{:S(2)}) collective-permute-start(bf16[2,256,16]{1,0,2:T(2,128)(2,1)S(1)} %collective-permute-done.6), channel_id=1, source_target_pairs={{0,4},{4,8},{8,12},{12,0},{1,5},{5,9},{9,13},{13,1},{2,6},{6,10},{... | collective-permute-start | bytes 49160 | tf_op jit(solution)/shard_map/ppermute | solution.py:34
  78.9 3.2 %collective-permute-start.9 = (bf16[1,256,16]{1,0,2:T(2,128)(2,1)S(1)}, bf16[1,256,16]{1,0,2:T(2,128)(2,1)S(1)}, u32[]{:S(2)}, u32[]{:S(2)}) collective-permute-start(bf16[1,256,16]{1,0,2:T(2,128)(2,1)S(1)} %fusion.90), channel_id=1, source_target_pairs={{0,4},{4,8},{8,12},{12,0},{1,5},{5,9},{9,13},{13,1},{2,6},{6,10},{... | collective-permute-start | bytes 24584 | tf_op jit(solution)/shard_map/ppermute | solution.py:34
  79.3 2.9 %collective-permute-start.11 = (bf16[1,256,16]{1,0,2:T(2,128)(2,1)S(1)}, bf16[1,256,16]{1,0,2:T(2,128)(2,1)S(1)}, u32[]{:S(2)}, u32[]{:S(2)}) collective-permute-start(bf16[1,256,16]{1,0,2:T(2,128)(2,1)S(1)} %fusion.90), channel_id=1, source_target_pairs={{4,0},{8,4},{12,8},{0,12},{5,1},{9,5},{13,9},{1,13},{6,2},{10,6},{... | collective-permute-start | bytes 24584 | tf_op jit(solution)/shard_map/ppermute | solution.py:40
  82.1 3.2 %collective-permute-start.10 = (bf16[1,256,16]{1,0,2:T(2,128)(2,1)S(1)}, bf16[1,256,16]{1,0,2:T(2,128)(2,1)S(1)}, u32[]{:S(2)}, u32[]{:S(2)}) collective-permute-start(bf16[1,256,16]{1,0,2:T(2,128)(2,1)S(1)} %collective-permute-done.9), channel_id=1, source_target_pairs={{0,4},{4,8},{8,12},{12,0},{1,5},{5,9},{9,13},{13,1},{2,6},{6,10},{... | collective-permute-start | bytes 24584 | tf_op jit(solution)/shard_map/ppermute | solution.py:34
  88.4 42.1 %reduce-scatter.15.cloned.1.call-start = ((), (), s32[]{:S(2)}) async-start(), calls=%async_computation.10 | async-start | bytes 81920 | tf_op jit(solution)/shard_map/reduce_scatter | solution.py:107
  110.3 53.2 %reduce-scatter.25.cloned.1.call-start = ((), (), s32[]{:S(2)}) async-start(), calls=%async_computation.15 | async-start | bytes 327680
  136.8 29.9 %copy-start.19 = (s32[4]{0:T(128)S(1)}, s32[4]{0:T(128)}, u32[]{:S(2)}) copy-start(s32[4]{0:T(128)} %get-tuple-element.15) | copy-start | bytes 52
  136.8 30.1 %copy-start.17 = (s32[4]{0:T(128)S(1)}, s32[4]{0:T(128)}, u32[]{:S(2)}) copy-start(s32[4]{0:T(128)} %copy-done.16) | copy-start | bytes 52
  143.3 47.1 %copy-start.9 = (bf16[4,256]{1,0:T(4,128)(2,1)S(1)}, bf16[4,256]{1,0:T(4,128)(2,1)}, u32[]{:S(2)}) copy-start(bf16[4,256]{1,0:T(4,128)(2,1)} %get-tuple-element.19) | copy-start | bytes 6148
  143.4 47.1 %reduce-scatter.17.cloned.1.call-start = ((), (), s32[]{:S(2)}) async-start(), calls=%async_computation.11 | async-start | bytes 163840 | tf_op jit(solution)/shard_map/reduce_scatter | solution.py:107
  166.9 46.0 %copy-start.6 = (f32[4,256]{1,0:T(4,128)S(1)}, f32[4,256]{1,0:T(4,128)}, u32[]{:S(2)}) copy-start(f32[4,256]{1,0:T(4,128)} %copy-done.5) | copy-start | bytes 12292
  167.2 51.3 %copy-start.15 = (s32[4]{0:T(128)S(1)}, s32[4]{0:T(128)}, u32[]{:S(2)}) copy-start(s32[4]{0:T(128)} %copy-done.14) | copy-start | bytes 52
  167.2 51.6 %copy-start.13 = (s32[4]{0:T(128)S(1)}, s32[4]{0:T(128)}, u32[]{:S(2)}) copy-start(s32[4]{0:T(128)} %copy-done.12) | copy-start | bytes 52
  167.2 51.8 %copy-start.11 = (s32[4]{0:T(128)S(1)}, s32[4]{0:T(128)}, u32[]{:S(2)}) copy-start(s32[4]{0:T(128)} %copy-done.10) | copy-start | bytes 52
  170.7 42.1 %reduce-scatter.19.cloned.1.call-start = ((), (), s32[]{:S(2)}) async-start(), calls=%async_computation.12 | async-start | bytes 163840 | tf_op jit(solution)/shard_map/reduce_scatter | solution.py:120
  193.1 51.2 %reduce-scatter.21.cloned.1.call-start = ((), (), s32[]{:S(2)}) async-start(), calls=%async_computation.13 | async-start | bytes 327680 | tf_op jit(solution)/shard_map/reduce_scatter | solution.py:107
  219.2 25.1 %copy-start.8 = (bf16[4,256]{1,0:T(4,128)(2,1)S(1)}, bf16[4,256]{1,0:T(4,128)(2,1)}, u32[]{:S(2)}) copy-start(bf16[4,256]{1,0:T(4,128)(2,1)} %get-tuple-element.2) | copy-start | bytes 6148
  219.4 47.5 %copy-start.4 = (f32[4,256]{1,0:T(4,128)S(1)}, f32[4,256]{1,0:T(4,128)}, u32[]{:S(2)}) copy-start(f32[4,256]{1,0:T(4,128)} %copy-done.3) | copy-start | bytes 12292
  224.1 42.7 %reduce-scatter.23.cloned.1.call-start = ((), (), s32[]{:S(2)}) async-start(), calls=%async_computation.14 | async-start | bytes 327680 | tf_op jit(solution)/shard_map/reduce_scatter | solution.py:120
Sparse Core Ops, SparseCore 0:
  31.8 10.9 reduce-scatter.10
  88.5 19.3 reduce-scatter.12
  111.0 19.4 reduce-scatter.14
  143.5 20.0 reduce-scatter.24
  170.8 19.5 reduce-scatter.16
  193.3 19.5 reduce-scatter.18
  224.2 20.0 reduce-scatter.20
  246.8 20.0 reduce-scatter.22
